TPU v7x, 32 devices: a whole 2x2x4 slice. The times are simulated.
32 devices in a mesh: lev: 4 (over x, core), tile: 8 (over z, y).
Axes of the slice: x: 2, y: 2, z: 4, core: 2. Of those that a mesh axis runs over, the one named last changes fastest.
Arguments:
- forcing: bfloat16 [4, 8, 36, 36, 128], P('lev', 'tile'), may hold values from -6 to 6
- transport: float32 [4, 4, 8, 36, 36], P(None, 'lev', 'tile'), may hold values from 0.04 to 0.22
- reactivity: float32 [4, 8, 36, 36], P('lev', 'tile'), may hold values from 0.1 to 0.6
- jacobian: float32 [4, 128, 128], P('lev'), may hold values from -0.5 to 0.5
- pattern: int32 [8, 8], replicated, may hold values 0 or 1
- lon_rate: float32 [128, 36], P('tile'), may hold values from 0.003 to 0.03
- lat_rate: float32 [128, 288], P('tile'), may hold values from 0.003 to 0.03
- vertical: float32 [128, 4, 4], replicated, may hold values from -3 to 3
- step_scale: float32 [128], replicated, may hold values from 0.3 to 1
- control: bfloat16 [4, 8, 36, 36, 128], P('lev', 'tile'), may hold values from -6 to 6
Outputs:
- control_new: bfloat16 [4, 8, 36, 36, 128], P('lev', 'tile')
All inputs are finite; a program needn't handle non-finite values.
Results may differ from a plain program's by a relative error of at most 0.001.
The roundings to bfloat16 on the way count: a program that leaves them out, or rounds other values in their place, can miss the bound.
Values may be sent and summed in bfloat16 or wider, within the bound.
A program may use at most 64 MiB of HBM per device.

v0:
```python
import functools

import jax
import jax.numpy as jnp
from jax import lax
from jax.experimental import pallas as pl
from jax.experimental.pallas import tpu as pltpu
from jax.sharding import PartitionSpec as P

TJ = 8
STEPS = 3


HIGHEST = lax.Precision.HIGHEST


def from_behind(x, axis, by):
    size = lax.axis_size(axis)
    return lax.ppermute(x, axis, [(i, (i + by) % size) for i in range(size)])


def neighbour_rim(edge, offset):
    return from_behind(edge, "tile", offset)


def filter_kernel(rates, blocks):
    cumulative = jnp.cumsum(rates)
    quarter = jnp.sqrt(jnp.sqrt(rates))
    kernel = (
        quarter[:, None]
        * quarter[None, :]
        * jnp.exp(-jnp.abs(cumulative[:, None] - cumulative[None, :]))
    )
    length = rates.shape[0] // blocks
    return kernel.reshape(blocks, length, blocks, length)


def on_device_general(
    forcing,
    transport,
    reactivity,
    jacobian,
    pattern,
    lon_rate,
    lat_rate,
    vertical,
    step_scale,
    control,
):
    adjoint = forcing[0, 0].astype(jnp.float32)
    tile_rows, tile_cols, species = adjoint.shape
    weights = transport[:, 0, 0]
    reacting = reactivity[0, 0][:, :, None]
    groups = pattern.shape[0]
    width = species // groups
    blockmask = jnp.broadcast_to(
        pattern.astype(jnp.float32)[:, None, :, None], (groups, width, groups, width)
    ).reshape(species, species)
    coupling = jacobian[0] * blockmask
    tiles = lax.axis_size("tile")
    lon_tiles = tiles // TJ
    placing = lax.axis_index("tile") % TJ
    keep_south = (placing > 0).astype(jnp.float32)
    keep_north = (placing < TJ - 1).astype(jnp.float32)
    for sweep in range(STEPS):
        if lon_tiles > 1:
            west_rim = neighbour_rim(adjoint[-1], TJ)
            east_rim = neighbour_rim(adjoint[0], -TJ)
        else:
            west_rim = adjoint[-1]
            east_rim = adjoint[0]
        south_rim = neighbour_rim(adjoint[:, -1], 1) * keep_south
        north_rim = neighbour_rim(adjoint[:, 0], -1) * keep_north
        from_west = jnp.concatenate([west_rim[None], adjoint[:-1]], 0)
        from_east = jnp.concatenate([adjoint[1:], east_rim[None]], 0)
        from_south = jnp.concatenate([south_rim[:, None], adjoint[:, :-1]], 1)
        from_north = jnp.concatenate([adjoint[:, 1:], north_rim[:, None]], 1)
        moved = (
            adjoint
            + weights[0][:, :, None] * (from_west - adjoint)
            + weights[1][:, :, None] * (from_east - adjoint)
            + weights[2][:, :, None] * (from_south - adjoint)
            + weights[3][:, :, None] * (from_north - adjoint)
        )
        reacted = jnp.dot(
            moved.reshape(tile_rows * tile_cols, species),
            coupling,
            precision=HIGHEST,
            preferred_element_type=jnp.float32,
        )
        adjoint = moved + reacting * reacted.reshape(tile_rows, tile_cols, species)
    gradient = adjoint.astype(jnp.bfloat16)
    planes = lax.all_to_all(
        gradient.reshape(1, tile_rows * tile_cols, species),
        "tile",
        split_axis=2,
        concat_axis=0,
        tiled=True,
    )
    owned = planes.shape[2]
    planes = jnp.moveaxis(planes.reshape(lon_tiles, TJ, tile_rows, tile_cols, owned), 4, 0)

    def filter_species(inputs):
        lon_line, lat_line, plane = inputs
        lon_kernel = filter_kernel(lon_line, lon_tiles)
        lat_kernel = filter_kernel(lat_line, TJ)
        along_lon = jnp.einsum(
            "abcd,cjdy->ajby", lon_kernel, plane.astype(jnp.float32), precision=HIGHEST
        )
        return jnp.einsum("jykz,akbz->ajby", lat_kernel, along_lon, precision=HIGHEST).astype(
            jnp.bfloat16
        )

    filtered = jnp.moveaxis(lax.map(filter_species, (lon_rate, lat_rate, planes)), 0, 4)
    level_here = lax.axis_index("lev")
    mixing = lax.dynamic_index_in_dim(vertical, level_here, 1, keepdims=False)
    returned = lax.all_to_all(
        filtered.reshape(tiles, tile_rows * tile_cols, owned),
        "tile",
        split_axis=0,
        concat_axis=2,
        tiled=True,
    )
    factor = mixing.T
    summed = jnp.sum(
        lax.all_gather(returned, "lev", axis=0, tiled=True) * factor[:, None, :], axis=0
    )
    increment = summed.reshape(tile_rows, tile_cols, species)
    updated = control[0, 0].astype(jnp.float32) - step_scale * increment
    return updated.astype(jnp.bfloat16)[None, None]


MESH = pl.DeviceIdType.MESH
RIM = STEPS
CHUNK = 10
GROUP = 8


def up_to(size, multiple):
    return -(-size // multiple) * multiple


def fused_kernel(tiles, levels, *refs):
    inputs, out_ref, held, arrived = refs[:10], refs[10], refs[11:21], refs[21]
    (
        forcing_ref,
        transport_ref,
        reactivity_ref,
        jacobian_ref,
        pattern_ref,
        lon_rate_ref,
        lat_rate_ref,
        vertical_ref,
        step_scale_ref,
        control_ref,
    ) = held
    (
        state_a,
        state_b,
        weights_own,
        weights_out,
        weights_rim,
        rim_out,
        rim_in,
        weights,
        moved_ref,
        split_ref,
        plane,
        ahead_ref,
        rates_own,
        rates_all,
        carry_out,
        carry_in,
        plane_far,
        lines_own,
        lines_far,
        grad_out,
        grad_in,
        fields,
        halo_send,
        halo_recv,
        rim_send,
        rim_recv,
        rate_send,
        rate_recv,
        carry_send,
        carry_recv,
        grad_send,
        grad_recv,
        both_send,
        both_recv,
        level_send,
        level_recv,
    ) = refs[22:]
    loads = [
        pltpu.make_async_copy(source, target, arrived.at[k])
        for k, (source, target) in enumerate(zip(inputs, held))
    ]
    for load in loads:
        load.start()
    nlon, nlat, species = forcing_ref.shape
    pitch = state_a.shape[1]
    rows = nlat + 2 * RIM
    rim_rows = rim_out.shape[1]
    owned, lat_total = lat_rate_ref.shape
    lon_at = lat_total
    rate_width = rates_own.shape[1]
    t = lax.axis_index("tile")
    level = lax.axis_index("lev")
    sibling = level + 1 - 2 * lax.rem(level, 2)
    across = lax.rem(level + 2, levels)
    f32, bf16 = jnp.float32, jnp.bfloat16

    barrier = pltpu.get_barrier_semaphore()
    for o in range(1, tiles):
        pl.semaphore_signal(
            barrier, inc=1, device_id=(level, lax.rem(t + o, tiles)), device_id_type=MESH
        )
    for other in (sibling, across):
        pl.semaphore_signal(barrier, inc=1, device_id=(other, t), device_id_type=MESH)

    weights_own[...] = jnp.zeros_like(weights_own)
    rates_own[...] = jnp.zeros_like(rates_own)
    plane[...] = jnp.zeros_like(plane)
    for load in loads[:-1]:
        load.wait()
    weights_own[0:4, 0:nlon, 0:nlat] = transport_ref[...].reshape(4, nlon, nlat)
    weights_own[4, 0:nlon, 0:nlat] = reactivity_ref[...].reshape(nlon, nlat)
    lane = lax.broadcasted_iota(jnp.int32, (pitch, 128), 1)
    thin = RIM - 1
    for side, first in ((0, nlat - thin), (1, 0)):
        packed = jnp.zeros((pitch, 128), f32)
        for d in range(5):
            moved_lanes = pltpu.roll(weights_own[d], (thin * d - first) % 128, 1)
            packed = jnp.where(lane // thin == d, moved_lanes, packed)
        weights_out[side] = packed
    rates_own[:, 0:lat_total] = lat_rate_ref[...]
    rates_own[:, lon_at : lon_at + nlon] = lon_rate_ref[...]
    for i in range(nlon):
        plane[i * pitch : i * pitch + nlat, :] = forcing_ref[i].astype(f32)
    plane[nlon * pitch : nlon * pitch + nlat, :] = forcing_ref[0].astype(f32)
    plane[(pitch - 1) * pitch : (pitch - 1) * pitch + nlat, :] = forcing_ref[nlon - 1].astype(f32)
    for j in range(nlat):
        state_a[RIM + j] = plane[pl.ds(j, pitch, stride=pitch), :]
    for side, first in ((0, nlat), (1, RIM)):
        rim_out[side] = jnp.concatenate(
            [
                state_a[first : first + RIM].reshape(RIM * pitch, species),
                jnp.zeros((rim_rows - RIM * pitch, species), f32),
            ],
            0,
        ).astype(bf16)

    pl.semaphore_wait(barrier, tiles + 1)

    def halo(side):
        place = t + 1 - 2 * side
        return (
            pltpu.make_async_remote_copy(
                src_ref=rim_out.at[side],
                dst_ref=rim_in.at[side],
                send_sem=halo_send.at[side],
                recv_sem=halo_recv.at[side],
                device_id=(level, place),
                device_id_type=MESH,
            ),
            pltpu.make_async_remote_copy(
                src_ref=weights_out.at[side],
                dst_ref=weights_rim.at[side],
                send_sem=rim_send.at[side],
                recv_sem=rim_recv.at[side],
                device_id=(level, place),
                device_id_type=MESH,
            ),
        )

    sends = [halo(0), halo(1)]

    @pl.when(t < tiles - 1)
    def _():
        for copy in sends[0]:
            copy.start()

    @pl.when(t > 0)
    def _():
        for copy in sends[1]:
            copy.start()

    @pl.when(t == 0)
    def _():
        rim_in[0] = jnp.zeros(rim_in.shape[1:], bf16)
        weights_rim[0] = jnp.zeros(weights_rim.shape[1:], f32)

    @pl.when(t == tiles - 1)
    def _():
        rim_in[1] = jnp.zeros(rim_in.shape[1:], bf16)
        weights_rim[1] = jnp.zeros(weights_rim.shape[1:], f32)

    mine = pl.ds(pl.multiple_of(t * owned, owned), owned)
    rate_copies = []
    for o in range(1, tiles):
        rate_copies.append(
            pltpu.make_async_remote_copy(
                src_ref=rates_own,
                dst_ref=rates_all.at[mine],
                send_sem=rate_send.at[o - 1],
                recv_sem=rate_recv.at[o - 1],
                device_id=(level, lax.rem(t + o, tiles)),
                device_id_type=MESH,
            )
        )
        rate_copies[-1].start()
    rates_all[mine, :] = rates_own[...]

    for j in range(nlat):
        weights[:, RIM + j] = jnp.broadcast_to(
            weights_own[:, :, j : j + 1], (5, pitch, species)
        )

    groups = pattern_ref.shape[0]
    width = species // groups
    member = (
        lax.broadcasted_iota(jnp.int32, (species, groups), 0) // width
        == lax.broadcasted_iota(jnp.int32, (species, groups), 1)
    ).astype(f32)
    mask = lax.dot_general(
        jnp.dot(member, pattern_ref[...].astype(f32), preferred_element_type=f32),
        member,
        (((1,), (1,)), ((), ())),
        preferred_element_type=f32,
    )
    coupling = jacobian_ref[...] * mask
    high = coupling.astype(bf16)
    low = (coupling - high.astype(f32)).astype(bf16)
    both = jnp.concatenate(
        [
            jnp.concatenate([high, low], 1),
            jnp.concatenate([high, jnp.zeros_like(low)], 1),
        ],
        0,
    )

    sums = [jnp.zeros((pitch, species), f32)] * 2

    def step(source, target, first, final, begin, end):
        chunk = GROUP if final else CHUNK
        for j0 in range(begin, end, chunk):
            n = min(chunk, end - j0)
            for j in range(j0, j0 + n, 2):
                here = source[j : j + 2]
                moved = (
                    here
                    + weights[0, j : j + 2] * (pltpu.roll(here, 1, 1) - here)
                    + weights[1, j : j + 2] * (pltpu.roll(here, pitch - 1, 1) - here)
                    + weights[2, j : j + 2] * (source[j - 1 : j + 1] - here)
                    + weights[3, j : j + 2] * (source[j + 1 : j + 3] - here)
                )
                moved = moved.reshape(2 * pitch, species)
                at = pl.ds((j - first) * pitch, 2 * pitch)
                moved_ref[at, :] = moved
                top = moved.astype(bf16)
                split_ref[at, 0:species] = top
                split_ref[at, species:] = (moved - top.astype(f32)).astype(bf16)
            at = pl.ds((j0 - first) * pitch, n * pitch)
            product = jnp.dot(split_ref[at, :], both, preferred_element_type=f32)
            reacted = product[:, :species] + product[:, species:]
            after = moved_ref[at, :].reshape(n, pitch, species) + weights[
                4, j0 : j0 + n
            ] * reacted.reshape(n, pitch, species)
            if final:
                rounded = after.reshape(n * pitch, species).astype(bf16)
                plane[at, :] = rounded.astype(f32)
                grad_out[at, :] = rounded
                grad_copies[(j0 - first) // GROUP].start()
                for j in range(j0 - first, j0 - first + n):
                    line = rounded[(j - j0 + first) * pitch : (j - j0 + first + 1) * pitch]
                    line = line.astype(f32)
                    sums[0] = sums[0] + to_north[j : j + 1] * line
                    sums[1] = sums[1] + to_south[j : j + 1] * line
            else:
                target[j0 : j0 + n] = after
                target[j0 : j0 + n, nlon : nlon + 1] = after[:, 0:1]
                target[j0 : j0 + n, pitch - 1 : pitch] = after[:, nlon - 1 : nlon]

    groups_at = [(k, min(GROUP, nlat - k)) for k in range(0, nlat, GROUP)]

    def rows_of(k):
        return pl.ds(groups_at[k][0] * pitch, groups_at[k][1] * pitch)

    grad_copies = [
        pltpu.make_async_remote_copy(
            src_ref=grad_out.at[rows_of(k)],
            dst_ref=grad_in.at[rows_of(k)],
            send_sem=grad_send.at[k],
            recv_sem=grad_recv.at[k],
            device_id=(across, t),
            device_id_type=MESH,
        )
        for k in range(len(groups_at))
    ]
    spare = pl.ds((nlat + 2) * pitch, (pitch - nlat - 2) * pitch)
    for buffer in (plane, plane_far):
        buffer[spare, :] = jnp.zeros(((pitch - nlat - 2) * pitch, species), f32)
    spare = pl.ds(nlon * pitch, (pitch - nlon) * pitch)
    for buffer in (lines_own, lines_far):
        buffer[spare, :] = jnp.zeros(((pitch - nlon) * pitch, species), f32)

    states = [state_a, state_b]
    low, top = 1, rows - 1
    step(state_a, state_b, low, False, low + RIM + 1, top - RIM - 1)

    @pl.when(t > 0)
    def _():
        sends[0][0].wait_recv()
        sends[0][1].wait_recv()

    @pl.when(t < tiles - 1)
    def _():
        sends[1][0].wait_recv()
        sends[1][1].wait_recv()

    for side, first in ((0, 0), (1, nlat + RIM)):
        rim = rim_in[side].astype(f32)[: RIM * pitch]
        state_a[first : first + RIM] = rim.reshape(RIM, pitch, species)
        for r in range(thin):
            for d in range(5):
                at = thin * d + r
                weights[d, (1, nlat + RIM)[side] + r] = jnp.broadcast_to(
                    weights_rim[side, :, at : at + 1], (pitch, species)
                )

    step(state_a, state_b, low, False, low, low + RIM + 1)
    step(state_a, state_b, low, False, top - RIM - 1, top)

    for copy in rate_copies:
        copy.wait()
    cell = lax.broadcasted_iota(jnp.int32, (pitch, rate_width), 1)
    row = lax.broadcasted_iota(jnp.int32, (pitch, rate_width), 0)
    start = t * nlat
    lat_cell = cell < lat_total
    picks = jnp.concatenate(
        [
            (cell == start + row) & (row < nlat),
            (cell >= start) & (cell <= start + row) & (cell < start + nlat),
            (cell < row * nlat) & lat_cell,
            (cell == lon_at + row) & (row < nlon),
        ],
        0,
    ).astype(f32)
    lines = lax.dot_general(
        picks,
        rates_all[...],
        (((1,), (1,)), ((), ())),
        precision=HIGHEST,
        preferred_element_type=f32,
    )
    lat_line = lines[0:pitch]
    lat_sum = lines[pitch : 2 * pitch]
    before = lines[2 * pitch : 3 * pitch]
    lon_line = lines[3 * pitch :]
    lat_q, lat_d = jnp.sqrt(jnp.sqrt(lat_line)), jnp.exp(-lat_line)
    lon_q, lon_d = jnp.sqrt(jnp.sqrt(lon_line)), jnp.exp(-lon_line)

    to_north = lat_q * jnp.exp(lat_sum - lat_sum[nlat - 1 : nlat])
    to_south = lat_q * jnp.exp(-lat_sum)

    for sweep in range(1, STEPS):
        step(
            states[sweep % 2],
            states[(sweep + 1) % 2],
            1 + sweep,
            sweep == STEPS - 1,
            1 + sweep,
            rows - 1 - sweep,
        )
    carry_out[0] = sums[0]
    carry_out[1] = sums[1]

    carry_copies = []
    for o in range(1, tiles):
        carry_copies.append(
            pltpu.make_async_remote_copy(
                src_ref=carry_out.at[(t + o) // tiles],
                dst_ref=carry_in.at[o - 1],
                send_sem=carry_send.at[o - 1],
                recv_sem=carry_recv.at[o - 1],
                device_id=(level, lax.rem(t + o, tiles)),
                device_id_type=MESH,
            )
        )
        carry_copies[-1].start()

    def along_lon(source, target, first, n):
        def item(i):
            cells = source[pl.ds(first * pitch + i, n, stride=pitch), :]
            return lon_q[i : i + 1] * cells

        carry = jnp.zeros((n, species), f32)
        for i in range(nlon):
            carry = item(i) + lon_d[i : i + 1] * carry
            target[pl.ds(i * pitch + first, n), :] = carry
        later = jnp.zeros((n, species), f32)
        for i in range(nlon - 1, -1, -1):
            at = pl.ds(i * pitch + first, n)
            target[at, :] = lon_q[i : i + 1] * (target[at, :] + later)
            later = lon_d[i : i + 1] * (item(i) + later)

    def take(k):
        grad_copies[k].wait_recv()
        plane_far[rows_of(k), :] = grad_in[rows_of(k), :].astype(f32)

    split_at = len(groups_at) - 2
    along_lon(plane, lines_own, 0, (len(groups_at) - 1) * GROUP)
    for begin, end in ((0, split_at - 1), (split_at - 1, split_at)):
        for k in range(begin, end):
            take(k)
        along_lon(plane_far, lines_far, begin * GROUP, (end - begin) * GROUP)

    order = lax.broadcasted_iota(jnp.int32, (pitch, species), 0)

    def before_tile(u):
        return jnp.sum(jnp.where(order == u, before, 0.0), 0, keepdims=True)

    south = jnp.zeros((pitch, species), f32)
    north = jnp.zeros((pitch, species), f32)
    for o in range(1, tiles):
        u = lax.rem(t + tiles - o, tiles)
        upper, lower = jnp.maximum(u, t), jnp.minimum(u, t)
        factor = jnp.exp(before_tile(lower + 1) - before_tile(upper))
        carry_copies[o - 1].wait()
        term = factor * carry_in[o - 1]
        south = south + jnp.where(o <= t, term, 0.0)
        north = north + jnp.where(o <= t, 0.0, term)
    plane[nlat * pitch : (nlat + 1) * pitch, :] = south
    plane[(nlat + 1) * pitch : (nlat + 2) * pitch, :] = north
    carried = pl.ds(nlat * pitch, 2 * pitch)
    both_copy = pltpu.make_async_remote_copy(
        src_ref=plane.at[carried],
        dst_ref=plane_far.at[carried],
        send_sem=both_send,
        recv_sem=both_recv,
        device_id=(across, t),
        device_id_type=MESH,
    )
    both_copy.start()

    def along_lat(lines_ref, slot):
        def line(j):
            return lines_ref[pl.ds(j, pitch, stride=pitch), :]

        carry = line(nlat)
        for j in range(nlat):
            carry = lat_q[j : j + 1] * line(j) + lat_d[j : j + 1] * carry
            ahead_ref[j] = carry
        later = line(nlat + 1)
        copies = {}
        for k in range(len(groups_at) - 1, -1, -1):
            first, n = groups_at[k]
            for j in range(first + n - 2, first - 1, -2):
                done = []
                for row_at in (j + 1, j):
                    q = lat_q[row_at : row_at + 1]
                    done.append(q * (ahead_ref[row_at] + later))
                    later = lat_d[row_at : row_at + 1] * (q * line(row_at) + later)
                fields[slot, pl.ds(j * pitch, 2 * pitch), :] = jnp.concatenate(
                    done[::-1], 0
                ).astype(bf16)
            copies[k] = pltpu.make_async_remote_copy(
                src_ref=fields.at[slot, rows_of(k)],
                dst_ref=fields.at[slot + 1, rows_of(k)],
                send_sem=level_send.at[slot // 2, k],
                recv_sem=level_recv.at[slot // 2, k],
                device_id=(sibling, t),
                device_id_type=MESH,
            )
            copies[k].start()
        return copies

    last_group = len(groups_at) - 1
    along_lon(plane, lines_own, last_group * GROUP, pitch - last_group * GROUP)
    near = along_lat(lines_own, 0)
    for k in range(split_at, len(groups_at)):
        take(k)
    both_copy.wait_recv()
    along_lon(plane_far, lines_far, split_at * GROUP, pitch - split_at * GROUP)
    relay = along_lat(lines_far, 2)

    loads[-1].wait()
    factors = [
        vertical_ref[level, pl.ds(source, 1), :]
        for source in (level, sibling, across, lax.rem(sibling + 2, levels))
    ]
    scale = step_scale_ref[...]
    for k in range(last_group, -1, -1):
        near[k].wait_recv()
        relay[k].wait_recv()
        at = rows_of(k)
        total = factors[0] * fields[0, at, :].astype(f32)
        for slot in range(1, levels):
            total = total + factors[slot] * fields[slot, at, :].astype(f32)
        moved_ref[at, :] = scale * total
    for i in range(nlon):
        total = moved_ref[pl.ds(i, pitch, stride=pitch), :]
        out_ref[i] = (control_ref[i].astype(f32) - total[:nlat]).astype(bf16)
    @pl.when(t < tiles - 1)
    def _():
        sends[0][0].wait_send()
        sends[0][1].wait_send()

    @pl.when(t > 0)
    def _():
        sends[1][0].wait_send()
        sends[1][1].wait_send()

    both_copy.wait_send()
    for k in range(len(groups_at)):
        grad_copies[k].wait_send()
        near[k].wait_send()
        relay[k].wait_send()


def on_device_fused(
    tiles,
    levels,
    forcing,
    transport,
    reactivity,
    jacobian,
    pattern,
    lon_rate,
    lat_rate,
    vertical,
    step_scale,
    control,
):
    nlon, nlat, species = forcing.shape[2:]
    pitch = up_to(max(nlon + 2, nlat), 8)
    rows = nlat + 2 * RIM
    owned, lat_total = lat_rate.shape
    rate_width = up_to(lat_total + nlon, 128)
    f32, bf16 = jnp.float32, jnp.bfloat16
    dma = pltpu.SemaphoreType.DMA
    count = -(-nlat // GROUP)
    rim_rows = up_to(RIM * pitch, 16)
    inputs = (
        forcing[0, 0],
        transport[:, 0, 0][:, :, None],
        reactivity[0, 0][:, None],
        jacobian[0],
        pattern,
        lon_rate,
        lat_rate,
        jnp.transpose(vertical, (1, 2, 0)),
        step_scale[None],
        control[0, 0],
    )
    updated = pl.pallas_call(
        functools.partial(fused_kernel, tiles, levels),
        out_shape=jax.ShapeDtypeStruct((nlon, nlat, species), bf16),
        in_specs=[pl.BlockSpec(memory_space=pltpu.HBM)] * 10,
        out_specs=pl.BlockSpec(memory_space=pltpu.VMEM),
        scratch_shapes=[pltpu.VMEM(x.shape, x.dtype) for x in inputs]
        + [
            dma((len(inputs),)),
            pltpu.VMEM((rows, pitch, species), f32),
            pltpu.VMEM((rows, pitch, species), f32),
            pltpu.VMEM((5, pitch, 128), f32),
            pltpu.VMEM((2, pitch, 128), f32),
            pltpu.VMEM((2, pitch, 128), f32),
            pltpu.VMEM((2, rim_rows, species), bf16),
            pltpu.VMEM((2, rim_rows, species), bf16),
            pltpu.VMEM((5, rows, pitch, species), f32),
            pltpu.VMEM((rows * pitch, species), f32),
            pltpu.VMEM((rows * pitch, 2 * species), bf16),
            pltpu.VMEM((pitch * pitch, species), f32),
            pltpu.VMEM((pitch, pitch, species), f32),
            pltpu.VMEM((owned, rate_width), f32),
            pltpu.VMEM((species, rate_width), f32),
            pltpu.VMEM((2, pitch, species), f32),
            pltpu.VMEM((tiles - 1, pitch, species), f32),
            pltpu.VMEM((pitch * pitch, species), f32),
            pltpu.VMEM((pitch * pitch, species), f32),
            pltpu.VMEM((pitch * pitch, species), f32),
            pltpu.VMEM((nlat * pitch, species), bf16),
            pltpu.VMEM((nlat * pitch, species), bf16),
            pltpu.VMEM((levels, nlat * pitch, species), bf16),
            dma((2,)),
            dma((2,)),
            dma((2,)),
            dma((2,)),
            dma((tiles - 1,)),
            dma((tiles - 1,)),
            dma((tiles - 1,)),
            dma((tiles - 1,)),
            dma((count,)),
            dma((count,)),
            dma,
            dma,
            dma((2, count)),
            dma((2, count)),
        ],
        compiler_params=pltpu.CompilerParams(
            collective_id=0, has_side_effects=True, vmem_limit_bytes=54500 * 1024
        ),
        name="fused",
    )(*inputs)
    return updated[None, None]


def on_device(forcing, *others):
    tiles, levels = lax.axis_size("tile"), lax.axis_size("lev")
    nlon, nlat, species = forcing.shape[2:]
    one_ring = tiles == TJ and levels == 4
    fits = nlon == nlat and nlat % GROUP in (2, 4) and nlat > 3 * GROUP and nlat + 2 * RIM <= 128
    if one_ring and fits and species == 128:
        return on_device_fused(tiles, levels, forcing, *others)
    return on_device_general(forcing, *others)


def solution(mesh):
    in_specs = (
        P("lev", "tile", None, None, None),
        P(None, "lev", "tile", None, None),
        P("lev", "tile", None, None),
        P("lev", None, None),
        P(),
        P("tile", None),
        P("tile", None),
        P(),
        P(),
        P("lev", "tile", None, None, None),
    )
    out_specs = P("lev", "tile", None, None, None)
    return jax.shard_map(
        on_device, mesh=mesh, in_specs=in_specs, out_specs=out_specs, check_vma=False
    )
```

profile of v0, /device:TPU:5, one launch (start us, length us, event | category | flops | bytes accessed | tf_op | source)
XLA Modules:
  0.0 31.0 jit_solution(14331576035177553133)
XLA Ops:
  0.0 0.0 copy-start.4
  0.0 0.0 copy-start.6
  0.0 0.0 copy-start.7
  0.0 0.7 %copy-done.4 = f32[16,36]{1,0:T(8,128)S(1)} copy-done((f32[16,36]{1,0:T(8,128)S(1)}, f32[16,36]{1,0:T(8,128)}, u32[]{:S(2)}) %copy-start.4) | copy-done | bytes 2328
  0.7 0.0 copy-done.6
  0.7 0.0 copy-done.7
  0.7 0.0 copy-start
  0.7 0.9 %copy-done = f32[4,1,1,36,36]{4,2,3,1,0:T(1,128)S(1)} copy-done((f32[4,1,1,36,36]{4,2,3,1,0:T(1,128)S(1)}, f32[4,1,1,36,36]{4,2,3,1,0:T(1,128)}, u32[]{:S(2)}) %copy-start) | copy-done | bytes 20760
  1.6 0.0 copy-start.1
  1.6 0.8 %copy-done.1 = f32[1,128,128]{2,1,0:T(8,128)S(1)} copy-done((f32[1,128,128]{2,1,0:T(8,128)S(1)}, f32[1,128,128]{2,1,0:T(8,128)}, u32[]{:S(2)}) %copy-start.1) | copy-done | bytes 65560
  2.4 0.0 copy-start.2
  2.4 0.7 %copy-done.2 = f32[16,288]{1,0:T(8,128)S(1)} copy-done((f32[16,288]{1,0:T(8,128)S(1)}, f32[16,288]{1,0:T(8,128)}, u32[]{:S(2)}) %copy-start.2) | copy-done | bytes 18456
  3.2 0.0 copy-start.3
  3.2 0.7 %copy-done.3 = f32[1,1,36,36]{3,1,2,0:T(1,128)S(1)} copy-done((f32[1,1,36,36]{3,1,2,0:T(1,128)S(1)}, f32[1,1,36,36]{3,1,2,0:T(1,128)}, u32[]{:S(2)}) %copy-start.3) | copy-done | bytes 5208
  3.9 0.0 copy-start.5
  3.9 0.7 %copy-done.5 = f32[128,4,4]{0,2,1:T(4,128)S(1)} copy-done((f32[128,4,4]{0,2,1:T(4,128)S(1)}, f32[128,4,4]{0,2,1:T(4,128)}, u32[]{:S(2)}) %copy-start.5) | copy-done | bytes 8216
  4.6 25.6 %fused.1 = bf16[36,36,128]{2,1,0:T(8,128)(2,1)S(1)} custom-call(bf16[36,36,128]{2,1,0:T(8,128)(2,1)} %bitcast.14, f32[4,36,1,36]{3,2,1,0:T(1,128)S(1)} %bitcast.9, f32[36,1,36]{2,1,0:T(1,128)S(1)} %bitcast.11, f32[128,128]{1,0:T(8,128)S(1)} %bitcast.10, s32[8,8]{1,0:T(8,128)S(1)} %copy-done.6, f32[16,36]{1,0:T(8,128)S(1)} %copy-done.4, ...), custom_call_target="tpu_custom_call" | custom-call | tf_op jit(solution)/shard_map/fused/pallas_call | solution.py:657
  30.2 0.7 %copy.12 = bf16[1,1,36,36,128]{4,3,2,1,0:T(8,128)(2,1)} copy(bf16[1,1,36,36,128]{4,3,2,1,0:T(8,128)(2,1)S(1)} %bitcast.8) | data formatting | bytes 663552
Async XLA Ops:
  0.0 0.7 %copy-start.4 = (f32[16,36]{1,0:T(8,128)S(1)}, f32[16,36]{1,0:T(8,128)}, u32[]{:S(2)}) copy-start(f32[16,36]{1,0:T(8,128)} %refs_5_.1) | copy-start | bytes 6916
  0.0 0.7 %copy-start.6 = (s32[8,8]{1,0:T(8,128)S(1)}, s32[8,8]{1,0:T(8,128)}, u32[]{:S(2)}) copy-start(s32[8,8]{1,0:T(8,128)} %refs_4_.1) | copy-start | bytes 772
  0.0 0.7 %copy-start.7 = (f32[128]{0:T(128)S(1)}, f32[128]{0:T(128)}, u32[]{:S(2)}) copy-start(f32[128]{0:T(128)} %param.18) | copy-start | bytes 1540
  0.7 0.9 %copy-start = (f32[4,1,1,36,36]{4,2,3,1,0:T(1,128)S(1)}, f32[4,1,1,36,36]{4,2,3,1,0:T(1,128)}, u32[]{:S(2)}) copy-start(f32[4,1,1,36,36]{4,2,3,1,0:T(1,128)} %param.11) | copy-start | bytes 62212
  1.6 0.8 %copy-start.1 = (f32[1,128,128]{2,1,0:T(8,128)S(1)}, f32[1,128,128]{2,1,0:T(8,128)}, u32[]{:S(2)}) copy-start(f32[1,128,128]{2,1,0:T(8,128)} %param.13) | copy-start | bytes 196612
  2.4 0.7 %copy-start.2 = (f32[16,288]{1,0:T(8,128)S(1)}, f32[16,288]{1,0:T(8,128)}, u32[]{:S(2)}) copy-start(f32[16,288]{1,0:T(8,128)} %refs_6_.1) | copy-start | bytes 55300
  3.2 0.7 %copy-start.3 = (f32[1,1,36,36]{3,1,2,0:T(1,128)S(1)}, f32[1,1,36,36]{3,1,2,0:T(1,128)}, u32[]{:S(2)}) copy-start(f32[1,1,36,36]{3,1,2,0:T(1,128)} %param.12) | copy-start | bytes 15556
  3.9 0.7 %copy-start.5 = (f32[128,4,4]{0,2,1:T(4,128)S(1)}, f32[128,4,4]{0,2,1:T(4,128)}, u32[]{:S(2)}) copy-start(f32[128,4,4]{0,2,1:T(4,128)} %param.17) | copy-start | bytes 24580
where the time goes:
time: 31.4 us; the launch traced here: 31 us
  Pallas kernels  25.6 us (82%)
  local copies, waits for them, and re-layouts  5.32 us (17%)
    pallas_call x1, Pallas kernels, on_device_fused(): pl.pallas_call(functools.partial(fused_kernel, tiles, levels), out_shape=...  25.6 us
    unnamed x17, local copies, waits for them, and re-layouts  5.32 us

commit v1 on v0

--- a/solution.py
+++ b/solution.py
@@ -203,8 +203,9 @@
     rows = nlat + 2 * RIM
     rim_rows = rim_out.shape[1]
     owned, lat_total = lat_rate_ref.shape
-    lon_at = lat_total
-    rate_width = rates_own.shape[1]
+    lon_at = nlat
+    sums_at = nlat + nlon
+    rate_width = rates_own.shape[2]
     t = lax.axis_index("tile")
     level = lax.axis_index("lev")
     sibling = level + 1 - 2 * lax.rem(level, 2)
@@ -220,7 +221,6 @@
         pl.semaphore_signal(barrier, inc=1, device_id=(other, t), device_id_type=MESH)
 
     weights_own[...] = jnp.zeros_like(weights_own)
-    rates_own[...] = jnp.zeros_like(rates_own)
     plane[...] = jnp.zeros_like(plane)
     for load in loads[:-1]:
         load.wait()
@@ -234,8 +234,18 @@
             moved_lanes = pltpu.roll(weights_own[d], (thin * d - first) % 128, 1)
             packed = jnp.where(lane // thin == d, moved_lanes, packed)
         weights_out[side] = packed
-    rates_own[:, 0:lat_total] = lat_rate_ref[...]
-    rates_own[:, lon_at : lon_at + nlon] = lon_rate_ref[...]
+    rate_lane = lax.broadcasted_iota(jnp.int32, (owned, rate_width), 1)
+    running = jnp.zeros((owned, 1), f32)
+    sums_of = jnp.zeros((owned, rate_width), f32)
+    for u in range(tiles):
+        running = running + jnp.sum(
+            lat_rate_ref[:, u * nlat : (u + 1) * nlat], 1, keepdims=True
+        )
+        sums_of = jnp.where(rate_lane == sums_at + u + 1, running, sums_of)
+    for u in range(tiles):
+        rates_own[u] = sums_of
+        rates_own[u, :, 0:nlat] = lat_rate_ref[:, u * nlat : (u + 1) * nlat]
+        rates_own[u, :, lon_at : lon_at + nlon] = lon_rate_ref[...]
     for i in range(nlon):
         plane[i * pitch : i * pitch + nlat, :] = forcing_ref[i].astype(f32)
     plane[nlon * pitch : nlon * pitch + nlat, :] = forcing_ref[0].astype(f32)
@@ -301,7 +311,7 @@
     for o in range(1, tiles):
         rate_copies.append(
             pltpu.make_async_remote_copy(
-                src_ref=rates_own,
+                src_ref=rates_own.at[lax.rem(t + o, tiles)],
                 dst_ref=rates_all.at[mine],
                 send_sem=rate_send.at[o - 1],
                 recv_sem=rate_recv.at[o - 1],
@@ -310,7 +320,7 @@
             )
         )
         rate_copies[-1].start()
-    rates_all[mine, :] = rates_own[...]
+    rates_all[mine, :] = rates_own[t]
 
     for j in range(nlat):
         weights[:, RIM + j] = jnp.broadcast_to(
@@ -432,17 +442,26 @@
     step(state_a, state_b, low, False, low, low + RIM + 1)
     step(state_a, state_b, low, False, top - RIM - 1, top)
 
+    last_sweep = STEPS - 1
+    for sweep in range(1, last_sweep):
+        step(
+            states[sweep % 2],
+            states[(sweep + 1) % 2],
+            1 + sweep,
+            False,
+            1 + sweep,
+            rows - 1 - sweep,
+        )
+
     for copy in rate_copies:
         copy.wait()
     cell = lax.broadcasted_iota(jnp.int32, (pitch, rate_width), 1)
     row = lax.broadcasted_iota(jnp.int32, (pitch, rate_width), 0)
-    start = t * nlat
-    lat_cell = cell < lat_total
     picks = jnp.concatenate(
         [
-            (cell == start + row) & (row < nlat),
-            (cell >= start) & (cell <= start + row) & (cell < start + nlat),
-            (cell < row * nlat) & lat_cell,
+            (cell == row) & (row < nlat),
+            (cell <= row) & (cell < nlat),
+            (cell == sums_at + row) & (row <= tiles),
             (cell == lon_at + row) & (row < nlon),
         ],
         0,
@@ -464,15 +483,14 @@
     to_north = lat_q * jnp.exp(lat_sum - lat_sum[nlat - 1 : nlat])
     to_south = lat_q * jnp.exp(-lat_sum)
 
-    for sweep in range(1, STEPS):
-        step(
-            states[sweep % 2],
-            states[(sweep + 1) % 2],
-            1 + sweep,
-            sweep == STEPS - 1,
-            1 + sweep,
-            rows - 1 - sweep,
-        )
+    step(
+        states[last_sweep % 2],
+        None,
+        1 + last_sweep,
+        True,
+        1 + last_sweep,
+        rows - 1 - last_sweep,
+    )
     carry_out[0] = sums[0]
     carry_out[1] = sums[1]
 
@@ -601,7 +619,7 @@
         moved_ref[at, :] = scale * total
     for i in range(nlon):
         total = moved_ref[pl.ds(i, pitch, stride=pitch), :]
-        out_ref[i] = (control_ref[i].astype(f32) - total[:nlat]).astype(bf16)
+        out_ref[i] = control_ref[i].astype(f32) - total[:nlat]
     @pl.when(t < tiles - 1)
     def _():
         sends[0][0].wait_send()
@@ -637,7 +655,7 @@
     pitch = up_to(max(nlon + 2, nlat), 8)
     rows = nlat + 2 * RIM
     owned, lat_total = lat_rate.shape
-    rate_width = up_to(lat_total + nlon, 128)
+    rate_width = up_to(nlat + nlon + tiles + 1, 128)
     f32, bf16 = jnp.float32, jnp.bfloat16
     dma = pltpu.SemaphoreType.DMA
     count = -(-nlat // GROUP)
@@ -656,7 +674,7 @@
     )
     updated = pl.pallas_call(
         functools.partial(fused_kernel, tiles, levels),
-        out_shape=jax.ShapeDtypeStruct((nlon, nlat, species), bf16),
+        out_shape=jax.ShapeDtypeStruct((nlon, nlat, species), f32),
         in_specs=[pl.BlockSpec(memory_space=pltpu.HBM)] * 10,
         out_specs=pl.BlockSpec(memory_space=pltpu.VMEM),
         scratch_shapes=[pltpu.VMEM(x.shape, x.dtype) for x in inputs]
@@ -674,7 +692,7 @@
             pltpu.VMEM((rows * pitch, 2 * species), bf16),
             pltpu.VMEM((pitch * pitch, species), f32),
             pltpu.VMEM((pitch, pitch, species), f32),
-            pltpu.VMEM((owned, rate_width), f32),
+            pltpu.VMEM((tiles, owned, rate_width), f32),
             pltpu.VMEM((species, rate_width), f32),
             pltpu.VMEM((2, pitch, species), f32),
             pltpu.VMEM((tiles - 1, pitch, species), f32),
@@ -700,11 +718,11 @@
             dma((2, count)),
         ],
         compiler_params=pltpu.CompilerParams(
-            collective_id=0, has_side_effects=True, vmem_limit_bytes=54500 * 1024
+            collective_id=0, has_side_effects=True, vmem_limit_bytes=56 * 1024 * 1024
         ),
         name="fused",
     )(*inputs)
-    return updated[None, None]
+    return updated.astype(bf16)[None, None]
 
 
 def on_device(forcing, *others):

time: 31.4 us -> 27 us (0.86)
  local copies, waits for them, and re-layouts: 5.32 us -> 0 us
  other arithmetic: 0 us -> 1.9 us
  Pallas kernels: 25.6 us -> 24.9 us
    unnamed x17 -> x0, local copies, waits for them, and re-layouts: 5.32 us -> none
    broadcast_in_dim x0 -> x1, other arithmetic: none -> 1.9 us  [on_device_fused(): return updated.astype(bf16)[None, None]]
    pallas_call x1, Pallas kernels: 25.6 us -> 24.9 us  [on_device_fused(): pl.pallas_call(functools.partial(fused_kernel, tiles, levels), out_shape=...]
where the time goes in v1:
time: 27 us; the launch traced here: 26.8 us
  Pallas kernels  24.9 us (92%)
  other arithmetic  1.9 us (7%)
    pallas_call x1, Pallas kernels, on_device_fused(): pl.pallas_call(functools.partial(fused_kernel, tiles, levels), out_shape=...  24.9 us
    broadcast_in_dim x1, other arithmetic, on_device_fused(): return updated.astype(bf16)[None, None]  1.9 us

profile of v1, /device:TPU:5, one launch (start us, length us, event | category | flops | bytes accessed | tf_op | source)
XLA Modules:
  0.0 26.8 jit_solution(10032803329275636057)
XLA Ops:
  0.0 24.9 %fused.1 = f32[36,36,128]{2,1,0:T(8,128)} custom-call(bf16[36,36,128]{2,1,0:T(8,128)(2,1)} %bitcast.9, f32[4,36,1,36]{3,2,1,0:T(1,128)} %bitcast.11, f32[36,1,36]{2,1,0:T(1,128)} %bitcast.13, f32[128,128]{1,0:T(8,128)} %bitcast.12, s32[8,8]{1,0:T(8,128)} %refs_4_.1, f32[16,36]{1,0:T(8,128)} %refs_5_.1, f32[16,288]{1,0:T(8,128)} %refs_6_.1, ...), custom_call_target="tpu_custom_call" | custom-call | tf_op jit(solution)/shard_map/fused/pallas_call | solution.py:675
  24.9 1.9 %convert_bitcast_fusion = bf16[1,1,36,36,128]{4,3,2,1,0:T(8,128)(2,1)} fusion(f32[36,36,128]{2,1,0:T(8,128)} %fused.1), kind=kLoop, calls=%fused_computation | loop fusion | flops 165888 | bytes 995328 | tf_op jit(solution)/shard_map/broadcast_in_dim | solution.py:725

commit v2 on v1

--- a/solution.py
+++ b/solution.py
@@ -380,7 +380,11 @@
             if final:
                 rounded = after.reshape(n * pitch, species).astype(bf16)
                 plane[at, :] = rounded.astype(f32)
-                grad_out[at, :] = rounded
+                exact = rounded.astype(f32)
+                packed = [exact[r * pitch : r * pitch + nlon] for r in range(n)]
+                grad_out[sent_of((j0 - first) // GROUP), :] = jnp.concatenate(
+                    packed, 0
+                ).astype(bf16)
                 grad_copies[(j0 - first) // GROUP].start()
                 for j in range(j0 - first, j0 - first + n):
                     line = rounded[(j - j0 + first) * pitch : (j - j0 + first + 1) * pitch]
@@ -397,10 +401,13 @@
     def rows_of(k):
         return pl.ds(groups_at[k][0] * pitch, groups_at[k][1] * pitch)
 
+    def sent_of(k):
+        return pl.ds(groups_at[k][0] * nlon, groups_at[k][1] * nlon)
+
     grad_copies = [
         pltpu.make_async_remote_copy(
-            src_ref=grad_out.at[rows_of(k)],
-            dst_ref=grad_in.at[rows_of(k)],
+            src_ref=grad_out.at[sent_of(k)],
+            dst_ref=grad_in.at[sent_of(k)],
             send_sem=grad_send.at[k],
             recv_sem=grad_recv.at[k],
             device_id=(across, t),
@@ -525,7 +532,10 @@
 
     def take(k):
         grad_copies[k].wait_recv()
-        plane_far[rows_of(k), :] = grad_in[rows_of(k), :].astype(f32)
+        first, n = groups_at[k]
+        cells = grad_in[sent_of(k), :].astype(f32)
+        for r in range(n):
+            plane_far[pl.ds((first + r) * pitch, nlon), :] = cells[r * nlon : (r + 1) * nlon]
 
     split_at = len(groups_at) - 2
     along_lon(plane, lines_own, 0, (len(groups_at) - 1) * GROUP)
@@ -619,7 +629,7 @@
         moved_ref[at, :] = scale * total
     for i in range(nlon):
         total = moved_ref[pl.ds(i, pitch, stride=pitch), :]
-        out_ref[i] = control_ref[i].astype(f32) - total[:nlat]
+        out_ref[i] = (control_ref[i].astype(f32) - total[:nlat]).astype(bf16)
     @pl.when(t < tiles - 1)
     def _():
         sends[0][0].wait_send()
@@ -674,7 +684,7 @@
     )
     updated = pl.pallas_call(
         functools.partial(fused_kernel, tiles, levels),
-        out_shape=jax.ShapeDtypeStruct((nlon, nlat, species), f32),
+        out_shape=jax.ShapeDtypeStruct((nlon, nlat, species), bf16),
         in_specs=[pl.BlockSpec(memory_space=pltpu.HBM)] * 10,
         out_specs=pl.BlockSpec(memory_space=pltpu.VMEM),
         scratch_shapes=[pltpu.VMEM(x.shape, x.dtype) for x in inputs]
@@ -699,8 +709,8 @@
             pltpu.VMEM((pitch * pitch, species), f32),
             pltpu.VMEM((pitch * pitch, species), f32),
             pltpu.VMEM((pitch * pitch, species), f32),
-            pltpu.VMEM((nlat * pitch, species), bf16),
-            pltpu.VMEM((nlat * pitch, species), bf16),
+            pltpu.VMEM((nlat * nlon, species), bf16),
+            pltpu.VMEM((nlat * nlon, species), bf16),
             pltpu.VMEM((levels, nlat * pitch, species), bf16),
             dma((2,)),
             dma((2,)),
@@ -722,14 +732,14 @@
         ),
         name="fused",
     )(*inputs)
-    return updated.astype(bf16)[None, None]
+    return updated[None, None]
 
 
 def on_device(forcing, *others):
     tiles, levels = lax.axis_size("tile"), lax.axis_size("lev")
     nlon, nlat, species = forcing.shape[2:]
     one_ring = tiles == TJ and levels == 4
-    fits = nlon == nlat and nlat % GROUP in (2, 4) and nlat > 3 * GROUP and nlat + 2 * RIM <= 128
+    fits = nlon == nlat and nlat % GROUP in (2, 4) and nlat > 3 * GROUP and nlat * nlon % 16 == 0 and nlat + 2 * RIM <= 128
     if one_ring and fits and species == 128:
         return on_device_fused(tiles, levels, forcing, *others)
     return on_device_general(forcing, *others)

time: 27 us -> 26.1 us (0.967)
  other arithmetic: 1.9 us -> 0 us
  local copies, waits for them, and re-layouts: 0 us -> 1.76 us
  Pallas kernels: 24.9 us -> 24.2 us
    broadcast_in_dim x1 -> x0, other arithmetic: 1.9 us -> none  [on_device_fused(): return updated.astype(bf16)[None, None]]
    unnamed x0 -> x1, local copies, waits for them, and re-layouts: none -> 1.76 us
    pallas_call x1, Pallas kernels: 24.9 us -> 24.2 us  [on_device_fused(): pl.pallas_call(functools.partial(fused_kernel, tiles, levels), out_shape=...]
where the time goes in v2:
time: 26.1 us; the launch traced here: 26 us
  Pallas kernels  24.2 us (93%)
  local copies, waits for them, and re-layouts  1.76 us (7%)
    pallas_call x1, Pallas kernels, on_device_fused(): pl.pallas_call(functools.partial(fused_kernel, tiles, levels), out_shape=...  24.2 us
    unnamed x1, local copies, waits for them, and re-layouts  1.76 us

profile of v2, /device:TPU:5, one launch (start us, length us, event | category | flops | bytes accessed | tf_op | source)
XLA Modules:
  0.0 26.0 jit_solution(5812872124916367310)
XLA Ops:
  0.0 24.2 %fused.1 = bf16[36,36,128]{2,1,0:T(8,128)(2,1)} custom-call(bf16[36,36,128]{2,1,0:T(8,128)(2,1)} %bitcast.9, f32[4,36,1,36]{3,2,1,0:T(1,128)} %bitcast.11, f32[36,1,36]{2,1,0:T(1,128)} %bitcast.13, f32[128,128]{1,0:T(8,128)} %bitcast.12, s32[8,8]{1,0:T(8,128)} %refs_4_.1, f32[16,36]{1,0:T(8,128)} %refs_5_.1, f32[16,288]{1,0:T(8,128)} %refs_6_.1, ...), custom_call_target="tpu_custom_call" | custom-call | tf_op jit(solution)/shard_map/fused/pallas_call | solution.py:685
  24.2 1.8 %copy.12 = bf16[1,1,36,36,128]{4,3,2,1,0:T(8,128)(2,1)} copy(bf16[1,1,36,36,128]{4,3,2,1,0:T(8,128)(2,1)} %bitcast.8) | data formatting | bytes 663552
